TPU v7x, 128 devices: a whole 4x4x4 slice. The times are simulated.
128 devices in a mesh: tx: 8 (over x, core), ty: 16 (over z, y).
Axes of the slice: x: 4, y: 4, z: 4, core: 2. Of those that a mesh axis runs over, the one named last changes fastest.
Arguments:
- right_side: bfloat16 [524288, 512], P(('tx', 'ty')), may hold values from -6 to 6
- points: bfloat16 [8, 524288], P(None, ('tx', 'ty'))
- leaf_inverse: bfloat16 [2048, 256, 256], P(('tx', 'ty'))
- level_one: bfloat16 [256, 1024, 1024], P(('tx', 'ty'))
- second_level_coupling: bfloat16 [16, 2048, 2048], P('ty', 'tx')
- neighbours: int32 [2048, 8], P(('tx', 'ty')), may hold values from 0 to 2047, as said below
- counts: int32 [2048], P(('tx', 'ty')), may hold values from 1 to 8
- leaf_skeleton: int32 [2048, 128], P(('tx', 'ty')), may hold values from 0 to 255, as said below
- node_skeleton: int32 [256, 128], P(('tx', 'ty')), may hold values from 0 to 1023, as said below
Outputs:
- solution: float32 [524288, 512], P(('tx', 'ty'))
Inputs may be any that keep to these rules, and one draw needn't show every extreme that they name: Each leaf's neighbours are distinct leaves other than itself, in the same block of 256 consecutive leaves, within 8 leaves of it; slot 0 lies exactly 8 leaves away. `leaf_skeleton`: distinct within each leaf. `node_skeleton`: distinct within each node.
All inputs are finite; a program needn't handle non-finite values.
Results may differ from a plain program's by a relative error of at most 0.009.
Values may be sent and summed in bfloat16 or wider, within the bound.
A program may use at most 320 MiB of HBM per device.

v0:
```python
import functools
import math

import jax
import jax.numpy as jnp
from jax import lax
from jax.experimental import pallas as pl
from jax.experimental.pallas import tpu as pltpu
from jax.sharding import PartitionSpec as P

PTS = 256
DIM = 8
SK = 128
GROUP = 8
NBR = 8
WIN = 8
MESH = pl.DeviceIdType.MESH
F32 = jnp.float32
BF16 = jnp.bfloat16
LOG2E = math.log2(math.e)


def mm(a, b):
    return jnp.dot(a, b, preferred_element_type=F32)


def device_kernel(
    dims,
    rhs,
    pts,
    leaf_inv,
    level_one,
    coupling,
    neigh,
    counts,
    leaf_skel,
    node_skel,
    out,
    *scratch,
):
    leaves, nodes, widths, n_tx, n_ty = dims
    chunks = len(widths)
    starts = [sum(widths[:c]) for c in range(chunks)]
    ext, up, gath, top, scratch = (
        scratch[:chunks],
        scratch[chunks : 2 * chunks],
        scratch[2 * chunks : 3 * chunks],
        scratch[3 * chunks : 4 * chunks],
        scratch[4 * chunks :],
    )
    (
        weights,
        inv,
        lone,
        coup_rows,
        inv_cols,
        leaf_pick,
        node_pick,
        node_spread,
        p_right,
        p_left,
        p_from_left,
        p_from_right,
        v_ext,
        u_all,
        u_leaf,
        halo_send,
        halo_recv,
        pts_send,
        pts_recv,
        top_send,
        top_recv,
        own_sem,
        load_sem,
    ) = scratch
    tx = lax.axis_index("tx")
    ty = lax.axis_index("ty")
    right = lax.rem(ty + 1, n_ty)
    left = lax.rem(ty + n_ty - 1, n_ty)
    own_rows = leaves * PTS
    side = WIN * PTS
    half = side // 2
    node_rows = GROUP * SK

    barrier = pltpu.get_barrier_semaphore()
    for t in (left, right):
        pl.semaphore_signal(barrier, inc=1, device_id=(tx, t), device_id_type=MESH)
    for k in range(1, n_tx):
        pl.semaphore_signal(
            barrier, inc=1, device_id=(lax.rem(tx + k, n_tx), ty), device_id_type=MESH
        )
    pl.semaphore_wait(barrier, 2 + n_tx - 1)

    def halo(c):
        cols = pl.ds(starts[c], widths[c])
        return (
            pltpu.make_async_remote_copy(
                src_ref=rhs.at[pl.ds(leaves - WIN, WIN), :, cols],
                dst_ref=ext[c].at[pl.ds(0, WIN)],
                send_sem=halo_send.at[c, 0],
                recv_sem=halo_recv.at[c, 0],
                device_id=(tx, right),
                device_id_type=MESH,
            ),
            pltpu.make_async_remote_copy(
                src_ref=rhs.at[pl.ds(0, WIN), :, cols],
                dst_ref=ext[c].at[pl.ds(WIN + leaves, WIN)],
                send_sem=halo_send.at[c, 1],
                recv_sem=halo_recv.at[c, 1],
                device_id=(tx, left),
                device_id_type=MESH,
            ),
        )

    def points_halo():
        return (
            pltpu.make_async_remote_copy(
                src_ref=p_right,
                dst_ref=p_from_left,
                send_sem=pts_send.at[0],
                recv_sem=pts_recv.at[0],
                device_id=(tx, right),
                device_id_type=MESH,
            ),
            pltpu.make_async_remote_copy(
                src_ref=p_left,
                dst_ref=p_from_right,
                send_sem=pts_send.at[1],
                recv_sem=pts_recv.at[1],
                device_id=(tx, left),
                device_id_type=MESH,
            ),
        )

    def own(c):
        return pltpu.make_async_copy(
            rhs.at[:, :, pl.ds(starts[c], widths[c])],
            ext[c].at[pl.ds(WIN, leaves)],
            own_sem.at[c],
        )

    loads = (
        pltpu.make_async_copy(leaf_inv, inv, load_sem.at[0]),
        pltpu.make_async_copy(coupling.at[0], coup_rows, load_sem.at[1]),
        pltpu.make_async_copy(level_one, lone, load_sem.at[2]),
    )

    coords = pts[...].astype(F32)

    def two_rows(x):
        return jnp.concatenate([x[:, :half], x[:, half:]], axis=0).astype(BF16)

    p_right[...] = two_rows(coords[:, own_rows - side :])
    p_left[...] = two_rows(coords[:, :side])
    for copy in points_halo():
        copy.start()
    for c in range(chunks):
        for copy in halo(c):
            copy.start()
    for copy in loads:
        copy.start()
    for c in range(chunks):
        own(c).start()

    def tails(x, sign_rows):
        sq = jnp.sum(x * x, axis=0, keepdims=True) * (-0.5 / DIM)
        high = sq.astype(BF16).astype(F32)
        rest = sq - high
        mid = rest.astype(BF16).astype(F32)
        low = rest - mid
        row = lax.broadcasted_iota(jnp.int32, (8, x.shape[1]), 0)
        at = 3 * sign_rows
        parts = jnp.where(
            row == at, high, jnp.where(row == at + 1, mid, jnp.where(row == at + 2, low, 1.0))
        )
        return jnp.where(row < 6, parts, 0.0)

    def put_other(place, x):
        block = jnp.concatenate([x, tails(x, 0)], axis=0).astype(BF16)
        for j in range(x.shape[1] // PTS):
            v_ext[place + j] = block[:, j * PTS : (j + 1) * PTS]

    u_all[...] = jnp.concatenate([coords * (1.0 / DIM), tails(coords, 1)], axis=0)
    put_other(WIN, coords)

    loads[0].wait()

    def leaf_setup(i, _):
        rows = pl.ds(pl.multiple_of(i * PTS, PTS), PTS)
        u_leaf[i] = u_all[:, rows].T.astype(BF16)
        spot = lax.broadcasted_iota(jnp.int32, (PTS, SK), 0)
        spread = (spot == leaf_skel[pl.ds(i, 1), :]).astype(F32)
        leaf_pick[i] = spread.T.astype(BF16)
        inv_cols[i] = mm(inv[i], spread.astype(BF16)).astype(BF16)
        return 0

    lax.fori_loop(0, leaves, leaf_setup, 0)
    for n in range(nodes):
        spot = lax.broadcasted_iota(jnp.int32, (node_rows, SK), 0)
        spread = (spot == node_skel[pl.ds(n, 1), :]).astype(F32)
        node_spread[n] = spread.astype(BF16)
        node_pick[n] = spread.T.astype(BF16)

    for copy in points_halo():
        copy.wait()
    for block, place in ((p_from_left, 0), (p_from_right, WIN + leaves)):
        far = block[...].astype(F32)
        put_other(place, far[:DIM])
        put_other(place + WIN // 2, far[DIM:])

    base = (tx * n_ty + ty) * leaves - WIN

    def place_of(i, s):
        return jnp.clip(neigh[s, i] - base, 0, leaves + 2 * WIN - 1)

    def leaf_kernel(i, _):
        mine = u_leaf[i]
        live = counts[i]
        for s in range(NBR):
            other = v_ext[place_of(i, s)]
            near = jnp.exp2(mm(mine, other) * LOG2E)
            weights[i * NBR + s] = jnp.where(s < live, near, 0.0).astype(BF16)
        return 0

    lax.fori_loop(0, leaves, leaf_kernel, 0)

    def upward(c):
        cols = pl.ds(starts[c], widths[c])

        def leaf(i, _):
            total = mm(weights[i * NBR], ext[c][place_of(i, 0)])
            for s in range(1, NBR):
                total += mm(weights[i * NBR + s], ext[c][place_of(i, s)])
            mine = ext[c][WIN + i].astype(F32)
            resid = (mine - total * PTS ** (-0.5)).astype(BF16)
            z = mm(inv[i], resid)
            out[pl.ds(pl.multiple_of(i * PTS, PTS), PTS), cols] = z
            up[c][pl.ds(pl.multiple_of(i * SK, SK), SK), :] = mm(
                leaf_pick[i], z.astype(BF16)
            ).astype(BF16)
            return 0

        lax.fori_loop(0, leaves, leaf, 0)

    def gather(c):
        return [
            pltpu.make_async_remote_copy(
                src_ref=top[c],
                dst_ref=gath[c].at[pl.ds(pl.multiple_of(tx * nodes * SK, SK), nodes * SK), :],
                send_sem=top_send.at[c, k - 1],
                recv_sem=top_recv.at[c, k - 1],
                device_id=(lax.rem(tx + k, n_tx), ty),
                device_id_type=MESH,
            )
            for k in range(1, n_tx)
        ]

    def send_top(c):
        for n in range(nodes):
            block = mm(node_pick[n], up[c][pl.ds(n * node_rows, node_rows), :]).astype(BF16)
            top[c][pl.ds(n * SK, SK), :] = block
            gath[c][pl.ds(pl.multiple_of(tx * nodes * SK + n * SK, SK), SK), :] = block
        for copy in gather(c):
            copy.start()

    def downward(c):
        cols = pl.ds(starts[c], widths[c])
        for copy in gather(c):
            copy.wait()
        back = mm(coup_rows[...], gath[c][...])
        for n in range(nodes):
            part = back[n * SK : (n + 1) * SK]
            high = part.astype(BF16)
            low = (part - high.astype(F32)).astype(BF16)
            spread = mm(node_spread[n], high) + mm(node_spread[n], low)
            here = up[c][pl.ds(n * node_rows, node_rows), :].astype(F32)
            down = (here - spread).astype(BF16)
            coup = mm(lone[n], down).astype(BF16)
            for j in range(GROUP):
                i = n * GROUP + j
                rows = pl.ds(i * PTS, PTS)
                out[rows, cols] = out[rows, cols] - mm(
                    inv_cols[i], coup[j * SK : (j + 1) * SK]
                )

    def arrive(c):
        own(c).wait()
        for copy in halo(c):
            copy.wait()

    for c in range(chunks):
        arrive(c)
        upward(c)
        send_top(c)
        if c == 0:
            loads[1].wait()
            loads[2].wait()
        elif c < chunks - 1:
            downward(c - 1)
        if c == chunks - 2:
            downward(c)
    downward(chunks - 1)


def on_device(rhs, pts, leaf_inv, level_one, coupling, neigh, counts, leaf_skel, node_skel):
    rows, cols = rhs.shape
    leaves, nodes = leaf_inv.shape[0], level_one.shape[0]
    n_tx, n_ty = lax.axis_size("tx"), lax.axis_size("ty")
    widths = (128,) * (cols // 128)
    chunks = len(widths)
    side = WIN * PTS
    ext_leaves = leaves + 2 * WIN
    dma = pltpu.SemaphoreType.DMA
    scratch = (
        [pltpu.VMEM((ext_leaves, PTS, w), BF16) for w in widths]
        + [pltpu.VMEM((leaves * SK, w), BF16) for w in widths]
        + [pltpu.VMEM((n_tx * nodes * SK, w), BF16) for w in widths]
        + [pltpu.VMEM((nodes * SK, w), BF16) for w in widths]
        + [
            pltpu.VMEM((leaves * NBR, PTS, PTS), BF16),
            pltpu.VMEM(leaf_inv.shape, BF16),
            pltpu.VMEM(level_one.shape, BF16),
            pltpu.VMEM(coupling.shape[1:], BF16),
            pltpu.VMEM((leaves, PTS, SK), BF16),
            pltpu.VMEM((leaves, SK, PTS), BF16),
            pltpu.VMEM((nodes, SK, GROUP * SK), BF16),
            pltpu.VMEM((nodes, GROUP * SK, SK), BF16),
            pltpu.VMEM((2 * DIM, side // 2), BF16),
            pltpu.VMEM((2 * DIM, side // 2), BF16),
            pltpu.VMEM((2 * DIM, side // 2), BF16),
            pltpu.VMEM((2 * DIM, side // 2), BF16),
            pltpu.VMEM((ext_leaves, 2 * DIM, PTS), BF16),
            pltpu.VMEM((2 * DIM, rows), F32),
            pltpu.VMEM((leaves, PTS, 2 * DIM), BF16),
            dma((chunks, 2)),
            dma((chunks, 2)),
            dma((2,)),
            dma((2,)),
            dma((chunks, n_tx - 1)),
            dma((chunks, n_tx - 1)),
            dma((chunks,)),
            dma((3,)),
        ]
    )
    vmem = pl.BlockSpec(memory_space=pltpu.VMEM)
    smem = pl.BlockSpec(memory_space=pltpu.SMEM)
    hbm = pl.BlockSpec(memory_space=pltpu.HBM)
    return pl.pallas_call(
        functools.partial(device_kernel, (leaves, nodes, widths, n_tx, n_ty)),
        out_shape=pltpu.VMEM((rows, cols), F32),
        in_specs=[hbm, vmem, hbm, hbm, hbm, smem, smem, vmem, vmem],
        out_specs=vmem,
        scratch_shapes=scratch,
        compiler_params=pltpu.CompilerParams(
            collective_id=0, has_side_effects=True, vmem_limit_bytes=50 * 2**20
        ),
        cost_estimate=pl.CostEstimate(
            flops=2 * 6_500_000_000, bytes_accessed=20_000_000, transcendentals=8_400_000
        ),
    )(rhs.reshape(leaves, PTS, cols), pts, leaf_inv, level_one, coupling, neigh.T, counts, leaf_skel, node_skel)


def solution(mesh):
    return jax.shard_map(
        on_device,
        mesh=mesh,
        in_specs=(
            P(("tx", "ty"), None),
            P(None, ("tx", "ty")),
            P(("tx", "ty"), None, None),
            P(("tx", "ty"), None, None),
            P("ty", "tx", None),
            P(("tx", "ty"), None),
            P(("tx", "ty")),
            P(("tx", "ty"), None),
            P(("tx", "ty"), None),
        ),
        out_specs=P(("tx", "ty"), None),
        check_vma=False,
    )
```

profile of v0, /device:TPU:1, one launch (start us, length us, event | category | flops | bytes accessed | tf_op | source)
XLA Modules:
  0.0 106.8 jit_solution(6358928650337867687)
XLA Ops:
  0.0 103.4 %shard_map.91 = f32[4096,512]{1,0:T(8,128)S(1)} custom-call(bf16[16,256,512]{2,1,0:T(8,128)(2,1)} %bitcast.2, bf16[8,4096]{1,0:T(8,128)(2,1)} %pts.1, bf16[16,256,256]{2,1,0:T(8,128)(2,1)} %leaf_inv.1, bf16[2,1024,1024]{2,1,0:T(8,128)(2,1)} %level_one.1, bf16[1,256,2048]{2,1,0:T(8,128)(2,1)} %coupling.1, s32[8,16]{1,0:T(8,128)} %bitcast.3, s32[16]{0:T(128)} %counts.1, ...), custom_call_target="tpu_custom_call" | custom-call | flops 12999999488 | bytes 20000000 | tf_op jit(solution)/shard_map/pallas_call | solution.py:348
  103.4 3.4 %copy.11 = f32[4096,512]{1,0:T(8,128)} copy(f32[4096,512]{1,0:T(8,128)S(1)} %shard_map.91) | data formatting | bytes 16777216
where the time goes:
time: 107 us
  Pallas kernels  103 us (96%)
  local copies, waits for them, and re-layouts  3.4 us (3%)
    pallas_call x1, Pallas kernels, on_device(): pl.pallas_call(functools.partial(device_kernel, (leaves, nodes, widths, n...  103 us
    unnamed x1, local copies, waits for them, and re-layouts  3.4 us

commit v1 on v0

--- a/solution.py
+++ b/solution.py
@@ -14,6 +14,7 @@
 GROUP = 8
 NBR = 8
 WIN = 8
+WIDE = 256
 MESH = pl.DeviceIdType.MESH
 F32 = jnp.float32
 BF16 = jnp.bfloat16
@@ -38,17 +39,15 @@
     out,
     *scratch,
 ):
-    leaves, nodes, widths, n_tx, n_ty = dims
+    leaves, nodes, widths, pieces, n_tx, n_ty = dims
     chunks = len(widths)
     starts = [sum(widths[:c]) for c in range(chunks)]
-    ext, up, gath, top, scratch = (
-        scratch[:chunks],
-        scratch[chunks : 2 * chunks],
-        scratch[2 * chunks : 3 * chunks],
-        scratch[3 * chunks : 4 * chunks],
-        scratch[4 * chunks :],
-    )
+    groups = [scratch[k * chunks : (k + 1) * chunks] for k in range(5)]
+    from_left, from_right, up, gath, top = groups
+    scratch = scratch[5 * chunks :]
     (
+        mine,
+        slot_of,
         weights,
         inv,
         lone,
@@ -91,22 +90,25 @@
         )
     pl.semaphore_wait(barrier, 2 + n_tx - 1)
 
-    def halo(c):
+    def halo(c, p):
         cols = pl.ds(starts[c], widths[c])
+        size = WIN // pieces[c]
+        far = WIN - (p + 1) * size
+        near = p * size
         return (
             pltpu.make_async_remote_copy(
-                src_ref=rhs.at[pl.ds(leaves - WIN, WIN), :, cols],
-                dst_ref=ext[c].at[pl.ds(0, WIN)],
-                send_sem=halo_send.at[c, 0],
-                recv_sem=halo_recv.at[c, 0],
+                src_ref=rhs.at[pl.ds(leaves - WIN + far, size), :, cols],
+                dst_ref=from_left[c].at[pl.ds(far, size)],
+                send_sem=halo_send.at[c, p, 0],
+                recv_sem=halo_recv.at[c, p, 0],
                 device_id=(tx, right),
                 device_id_type=MESH,
             ),
             pltpu.make_async_remote_copy(
-                src_ref=rhs.at[pl.ds(0, WIN), :, cols],
-                dst_ref=ext[c].at[pl.ds(WIN + leaves, WIN)],
-                send_sem=halo_send.at[c, 1],
-                recv_sem=halo_recv.at[c, 1],
+                src_ref=rhs.at[pl.ds(near, size), :, cols],
+                dst_ref=from_right[c].at[pl.ds(near, size)],
+                send_sem=halo_send.at[c, p, 1],
+                recv_sem=halo_recv.at[c, p, 1],
                 device_id=(tx, left),
                 device_id_type=MESH,
             ),
@@ -132,12 +134,12 @@
             ),
         )
 
-    def own(c):
+    def own(h):
         return pltpu.make_async_copy(
-            rhs.at[:, :, pl.ds(starts[c], widths[c])],
-            ext[c].at[pl.ds(WIN, leaves)],
-            own_sem.at[c],
+            rhs.at[:, :, pl.ds(h * WIDE, WIDE)], mine.at[h, pl.ds(0, leaves)], own_sem.at[h]
         )
+
+    halves = mine.shape[0]
 
     loads = (
         pltpu.make_async_copy(leaf_inv, inv, load_sem.at[0]),
@@ -155,12 +157,15 @@
     for copy in points_halo():
         copy.start()
     for c in range(chunks):
-        for copy in halo(c):
-            copy.start()
+        for p in range(pieces[c]):
+            for copy in halo(c, p):
+                copy.start()
     for copy in loads:
         copy.start()
-    for c in range(chunks):
-        own(c).start()
+    for h in range(halves):
+        own(h).start()
+        mine[h, leaves] = jnp.zeros((PTS, WIDE), BF16)
+    weights[leaves * NBR] = jnp.zeros((PTS, PTS), BF16)
 
     def tails(x, sign_rows):
         sq = jnp.sum(x * x, axis=0, keepdims=True) * (-0.5 / DIM)
@@ -214,33 +219,85 @@
         return jnp.clip(neigh[s, i] - base, 0, leaves + 2 * WIN - 1)
 
     def leaf_kernel(i, _):
-        mine = u_leaf[i]
+        here = u_leaf[i]
         live = counts[i]
+        places = [place_of(i, s) for s in range(NBR)]
+        first = jnp.where(i < WIN, 0, WIN + leaves)
+        for h in range(WIN):
+            slot = leaves * NBR
+            for s in range(NBR):
+                hit = (places[s] == first + h) & (s < live)
+                slot = jnp.where(hit, i * NBR + s, slot)
+            slot_of[i * WIN + h] = slot
         for s in range(NBR):
-            other = v_ext[place_of(i, s)]
-            near = jnp.exp2(mm(mine, other) * LOG2E)
+            near = jnp.exp2(mm(here, v_ext[places[s]]) * LOG2E)
             weights[i * NBR + s] = jnp.where(s < live, near, 0.0).astype(BF16)
         return 0
 
     lax.fori_loop(0, leaves, leaf_kernel, 0)
 
+    def rows_of(i, size):
+        return pl.ds(pl.multiple_of(i * size, size), size)
+
+    def own_near(h):
+        cols = pl.ds(h * WIDE, WIDE)
+
+        def own_place(i, s):
+            at = place_of(i, s) - WIN
+            return jnp.where((at >= 0) & (at < leaves), at, leaves)
+
+        def leaf(i, _):
+            total = mm(weights[i * NBR], mine[h, own_place(i, 0)])
+            for s in range(1, NBR):
+                total += mm(weights[i * NBR + s], mine[h, own_place(i, s)])
+            out[rows_of(i, PTS), cols] = total
+            return 0
+
+        lax.fori_loop(0, leaves, leaf, 0, unroll=2)
+
     def upward(c):
         cols = pl.ds(starts[c], widths[c])
-
-        def leaf(i, _):
-            total = mm(weights[i * NBR], ext[c][place_of(i, 0)])
-            for s in range(1, NBR):
-                total += mm(weights[i * NBR + s], ext[c][place_of(i, s)])
-            mine = ext[c][WIN + i].astype(F32)
-            resid = (mine - total * PTS ** (-0.5)).astype(BF16)
-            z = mm(inv[i], resid)
-            out[pl.ds(pl.multiple_of(i * PTS, PTS), PTS), cols] = z
-            up[c][pl.ds(pl.multiple_of(i * SK, SK), SK), :] = mm(
-                leaf_pick[i], z.astype(BF16)
-            ).astype(BF16)
-            return 0
-
-        lax.fori_loop(0, leaves, leaf, 0)
+        h, lane = divmod(starts[c], WIDE)
+
+        def with_halo(i, block, places):
+            total = out[rows_of(i, PTS), cols]
+            for at in places:
+                total += mm(weights[slot_of[i * WIN + at]], block[at])
+            return total
+
+        for p in range(WIN // 2):
+            step = WIN // 2 // pieces[c]
+            if p % step == 0:
+                for copy in halo(c, p // step):
+                    copy.wait()
+            low, high = (WIN - 1 - 2 * p, WIN - 2 - 2 * p), (2 * p, 2 * p + 1)
+
+            def leaf(i, _):
+                j = leaves - 1 - i
+                a = with_halo(i, from_left[c], low)
+                b = with_halo(j, from_right[c], high)
+                out[rows_of(i, PTS), cols] = a
+                out[rows_of(j, PTS), cols] = b
+                return 0
+
+            if p < WIN // 2 - 1:
+                lax.fori_loop(0, WIN - 2 - 2 * p, leaf, 0)
+            done = (WIN - 1 - 2 * p, WIN - 2 - 2 * p, WIN + 2 * p, WIN + 2 * p + 1)
+            near = (
+                with_halo(done[0], from_left[c], low[:1]),
+                with_halo(done[1], from_left[c], low),
+                with_halo(done[2], from_right[c], high[:1]),
+                with_halo(done[3], from_right[c], high),
+            )
+            resid = [
+                (mine[h, i, :, lane : lane + widths[c]].astype(F32) - t * PTS ** (-0.5)).astype(BF16)
+                for i, t in zip(done, near)
+            ]
+            inner = [mm(inv[i], r) for i, r in zip(done, resid)]
+            for i, z in zip(done, inner):
+                out[pl.ds(i * PTS, PTS), cols] = z
+            for i, z in zip(done, inner):
+                up[c][pl.ds(i * SK, SK), :] = mm(leaf_pick[i], z.astype(BF16)).astype(BF16)
 
     def gather(c):
         return [
@@ -283,22 +340,18 @@
                     inv_cols[i], coup[j * SK : (j + 1) * SK]
                 )
 
-    def arrive(c):
-        own(c).wait()
-        for copy in halo(c):
-            copy.wait()
-
+    for h in range(halves):
+        own(h).wait()
+    for h in range(halves):
+        own_near(h)
     for c in range(chunks):
-        arrive(c)
         upward(c)
         send_top(c)
         if c == 0:
             loads[1].wait()
             loads[2].wait()
-        elif c < chunks - 1:
+        else:
             downward(c - 1)
-        if c == chunks - 2:
-            downward(c)
     downward(chunks - 1)
 
 
@@ -306,18 +359,21 @@
     rows, cols = rhs.shape
     leaves, nodes = leaf_inv.shape[0], level_one.shape[0]
     n_tx, n_ty = lax.axis_size("tx"), lax.axis_size("ty")
-    widths = (128,) * (cols // 128)
+    widths = (WIDE,) * (cols // WIDE - 1) + (WIDE // 2,) * 2
+    pieces = (1,) * (len(widths) - 1) + (4,)
     chunks = len(widths)
     side = WIN * PTS
-    ext_leaves = leaves + 2 * WIN
+    halves = cols // WIDE
     dma = pltpu.SemaphoreType.DMA
     scratch = (
-        [pltpu.VMEM((ext_leaves, PTS, w), BF16) for w in widths]
+        [pltpu.VMEM((WIN, PTS, w), BF16) for w in widths * 2]
         + [pltpu.VMEM((leaves * SK, w), BF16) for w in widths]
         + [pltpu.VMEM((n_tx * nodes * SK, w), BF16) for w in widths]
         + [pltpu.VMEM((nodes * SK, w), BF16) for w in widths]
         + [
-            pltpu.VMEM((leaves * NBR, PTS, PTS), BF16),
+            pltpu.VMEM((halves, leaves + 1, PTS, WIDE), BF16),
+            pltpu.SMEM((leaves * WIN,), jnp.int32),
+            pltpu.VMEM((leaves * NBR + 1, PTS, PTS), BF16),
             pltpu.VMEM(leaf_inv.shape, BF16),
             pltpu.VMEM(level_one.shape, BF16),
             pltpu.VMEM(coupling.shape[1:], BF16),
@@ -329,16 +385,16 @@
             pltpu.VMEM((2 * DIM, side // 2), BF16),
             pltpu.VMEM((2 * DIM, side // 2), BF16),
             pltpu.VMEM((2 * DIM, side // 2), BF16),
-            pltpu.VMEM((ext_leaves, 2 * DIM, PTS), BF16),
+            pltpu.VMEM((leaves + 2 * WIN, 2 * DIM, PTS), BF16),
             pltpu.VMEM((2 * DIM, rows), F32),
             pltpu.VMEM((leaves, PTS, 2 * DIM), BF16),
-            dma((chunks, 2)),
-            dma((chunks, 2)),
+            dma((chunks, max(pieces), 2)),
+            dma((chunks, max(pieces), 2)),
             dma((2,)),
             dma((2,)),
             dma((chunks, n_tx - 1)),
             dma((chunks, n_tx - 1)),
-            dma((chunks,)),
+            dma((halves,)),
             dma((3,)),
         ]
     )
@@ -346,7 +402,7 @@
     smem = pl.BlockSpec(memory_space=pltpu.SMEM)
     hbm = pl.BlockSpec(memory_space=pltpu.HBM)
     return pl.pallas_call(
-        functools.partial(device_kernel, (leaves, nodes, widths, n_tx, n_ty)),
+        functools.partial(device_kernel, (leaves, nodes, widths, pieces, n_tx, n_ty)),
         out_shape=pltpu.VMEM((rows, cols), F32),
         in_specs=[hbm, vmem, hbm, hbm, hbm, smem, smem, vmem, vmem],
         out_specs=vmem,

time: 107 us -> 82.8 us (0.77)
  Pallas kernels: 103 us -> 79.3 us
    pallas_call x1, Pallas kernels: 103 us -> 79.3 us  [on_device(): pl.pallas_call(functools.partial(device_kernel, (leaves, nodes, widths, p...]
where the time goes in v1:
time: 82.8 us; the launch traced here: 82.7 us
  Pallas kernels  79.3 us (96%)
  local copies, waits for them, and re-layouts  3.4 us (4%)
    pallas_call x1, Pallas kernels, on_device(): pl.pallas_call(functools.partial(device_kernel, (leaves, nodes, widths, p...  79.3 us
    unnamed x1, local copies, waits for them, and re-layouts  3.4 us

profile of v1, /device:TPU:1, one launch (start us, length us, event | category | flops | bytes accessed | tf_op | source)
XLA Modules:
  0.0 82.7 jit_solution(14967729784938925404)
XLA Ops:
  0.0 79.3 %shard_map.91 = f32[4096,512]{1,0:T(8,128)S(1)} custom-call(bf16[16,256,512]{2,1,0:T(8,128)(2,1)} %bitcast.2, bf16[8,4096]{1,0:T(8,128)(2,1)} %pts.1, bf16[16,256,256]{2,1,0:T(8,128)(2,1)} %leaf_inv.1, bf16[2,1024,1024]{2,1,0:T(8,128)(2,1)} %level_one.1, bf16[1,256,2048]{2,1,0:T(8,128)(2,1)} %coupling.1, s32[8,16]{1,0:T(8,128)} %bitcast.3, s32[16]{0:T(128)} %counts.1, ...), custom_call_target="tpu_custom_call" | custom-call | flops 12999999488 | bytes 20000000 | tf_op jit(solution)/shard_map/pallas_call | solution.py:404
  79.3 3.4 %copy.11 = f32[4096,512]{1,0:T(8,128)} copy(f32[4096,512]{1,0:T(8,128)S(1)} %shard_map.91) | data formatting | bytes 16777216

commit v2 on v1

--- a/solution.py
+++ b/solution.py
@@ -23,6 +23,42 @@
 
 def mm(a, b):
     return jnp.dot(a, b, preferred_element_type=F32)
+
+
+def rows_of(i, size):
+    return pl.ds(pl.multiple_of(i * size, size), size)
+
+
+def downward(nodes, coup_rows, gath, up, node_spread, lone, inv_cols, store):
+    width = up.shape[1]
+    back = mm(coup_rows[...], gath[...])
+    for n in range(nodes):
+        part = back[n * SK : (n + 1) * SK]
+        high = part.astype(BF16)
+        low = (part - high.astype(F32)).astype(BF16)
+        spread = mm(node_spread[n], jnp.concatenate([high, low], axis=0))
+        here = up[pl.ds(n * GROUP * SK, GROUP * SK), :].astype(F32)
+        down = (here - spread).astype(BF16)
+        coup = mm(lone[n], down).astype(BF16)
+        blocks = [coup[j * SK : (j + 1) * SK] for j in range(GROUP)]
+        for j in range(0, GROUP, 2):
+            i = n * GROUP + j
+            cols = inv_cols[i // 2]
+            if width <= SK:
+                none = jnp.zeros_like(blocks[j])
+                pair = jnp.concatenate(
+                    [
+                        jnp.concatenate([blocks[j], none], axis=1),
+                        jnp.concatenate([none, blocks[j + 1]], axis=1),
+                    ],
+                    axis=0,
+                )
+                both = mm(cols, pair)
+                store(i, both[:, :width])
+                store(i + 1, both[:, width:])
+            else:
+                store(i, mm(cols[:, :SK], blocks[j]))
+                store(i + 1, mm(cols[:, SK:], blocks[j + 1]))
 
 
 def device_kernel(
@@ -37,25 +73,31 @@
     leaf_skel,
     node_skel,
     out,
+    gath_last,
+    up_last,
+    coup_rows,
+    lone,
+    node_spread,
+    inv_cols,
     *scratch,
 ):
     leaves, nodes, widths, pieces, n_tx, n_ty = dims
     chunks = len(widths)
     starts = [sum(widths[:c]) for c in range(chunks)]
-    groups = [scratch[k * chunks : (k + 1) * chunks] for k in range(5)]
-    from_left, from_right, up, gath, top = groups
-    scratch = scratch[5 * chunks :]
+    groups = [scratch[k * chunks : (k + 1) * chunks] for k in range(3)]
+    from_left, from_right, top = groups
+    scratch = scratch[3 * chunks :]
+    up = scratch[: chunks - 1] + (up_last,)
+    gath = scratch[chunks - 1 : 2 * chunks - 2] + (gath_last,)
+    scratch = scratch[2 * chunks - 2 :]
     (
         mine,
+        held,
         slot_of,
         weights,
         inv,
-        lone,
-        coup_rows,
-        inv_cols,
         leaf_pick,
         node_pick,
-        node_spread,
         p_right,
         p_left,
         p_from_left,
@@ -84,11 +126,11 @@
     barrier = pltpu.get_barrier_semaphore()
     for t in (left, right):
         pl.semaphore_signal(barrier, inc=1, device_id=(tx, t), device_id_type=MESH)
-    for k in range(1, n_tx):
-        pl.semaphore_signal(
-            barrier, inc=1, device_id=(lax.rem(tx + k, n_tx), ty), device_id_type=MESH
-        )
-    pl.semaphore_wait(barrier, 2 + n_tx - 1)
+    mate = tx + 1 - 2 * lax.rem(tx, 2)
+    turns = n_tx // 2
+    for t in [mate] + [lax.rem(tx + 2 * k, n_tx) for k in range(1, turns)]:
+        pl.semaphore_signal(barrier, inc=1, device_id=(t, ty), device_id_type=MESH)
+    pl.semaphore_wait(barrier, 2 + turns)
 
     def halo(c, p):
         cols = pl.ds(starts[c], widths[c])
@@ -190,20 +232,23 @@
 
     loads[0].wait()
 
-    def leaf_setup(i, _):
-        rows = pl.ds(pl.multiple_of(i * PTS, PTS), PTS)
-        u_leaf[i] = u_all[:, rows].T.astype(BF16)
+    def leaf_setup(q, _):
         spot = lax.broadcasted_iota(jnp.int32, (PTS, SK), 0)
-        spread = (spot == leaf_skel[pl.ds(i, 1), :]).astype(F32)
-        leaf_pick[i] = spread.T.astype(BF16)
-        inv_cols[i] = mm(inv[i], spread.astype(BF16)).astype(BF16)
+        for k in range(2):
+            i = 2 * q + k
+            u_leaf[i] = u_all[:, rows_of(i, PTS)].T.astype(BF16)
+            spread = (spot == leaf_skel[pl.ds(i, 1), :]).astype(F32)
+            leaf_pick[i] = spread.T.astype(BF16)
+            cols = mm(inv[i], spread.astype(BF16)).astype(BF16)
+            inv_cols[q, :, k * SK : (k + 1) * SK] = cols
         return 0
 
-    lax.fori_loop(0, leaves, leaf_setup, 0)
+    lax.fori_loop(0, leaves // 2, leaf_setup, 0)
     for n in range(nodes):
         spot = lax.broadcasted_iota(jnp.int32, (node_rows, SK), 0)
         spread = (spot == node_skel[pl.ds(n, 1), :]).astype(F32)
-        node_spread[n] = spread.astype(BF16)
+        node_spread[n, :, :SK] = spread.astype(BF16)
+        node_spread[n, :, SK:] = spread.astype(BF16)
         node_pick[n] = spread.T.astype(BF16)
 
     for copy in points_halo():
@@ -234,10 +279,7 @@
             weights[i * NBR + s] = jnp.where(s < live, near, 0.0).astype(BF16)
         return 0
 
-    lax.fori_loop(0, leaves, leaf_kernel, 0)
-
-    def rows_of(i, size):
-        return pl.ds(pl.multiple_of(i * size, size), size)
+    lax.fori_loop(0, leaves, leaf_kernel, 0, unroll=2)
 
     def own_near(h):
         cols = pl.ds(h * WIDE, WIDE)
@@ -253,7 +295,7 @@
             out[rows_of(i, PTS), cols] = total
             return 0
 
-        lax.fori_loop(0, leaves, leaf, 0, unroll=2)
+        lax.fori_loop(0, leaves, leaf, 0, unroll=4)
 
     def upward(c):
         cols = pl.ds(starts[c], widths[c])
@@ -265,11 +307,24 @@
                 total += mm(weights[slot_of[i * WIN + at]], block[at])
             return total
 
+        def finish(done, near):
+            own_rhs = [mine[h, i, :, lane : lane + widths[c]].astype(F32) for i in done]
+            return [(r - t * PTS ** (-0.5)).astype(BF16) for r, t in zip(own_rhs, near)]
+
+        def inverse(done, resid):
+            inner = [mm(inv[i], r) for i, r in zip(done, resid)]
+            for i, z in zip(done, inner):
+                out[rows_of(i, PTS), cols] = z
+            for i, z in zip(done, inner):
+                up[c][rows_of(i, SK), :] = mm(leaf_pick[i], z.astype(BF16)).astype(BF16)
+
         for p in range(WIN // 2):
             step = WIN // 2 // pieces[c]
             if p % step == 0:
                 for copy in halo(c, p // step):
                     copy.wait()
+            if c > 0 and p == (0 if pieces[c] == 1 else WIN // 2 - 2):
+                pass_on(c - 1)
             low, high = (WIN - 1 - 2 * p, WIN - 2 - 2 * p), (2 * p, 2 * p + 1)
 
             def leaf(i, _):
@@ -281,7 +336,7 @@
                 return 0
 
             if p < WIN // 2 - 1:
-                lax.fori_loop(0, WIN - 2 - 2 * p, leaf, 0)
+                lax.fori_loop(0, WIN - 2 - 2 * p, leaf, 0, unroll=2)
             done = (WIN - 1 - 2 * p, WIN - 2 - 2 * p, WIN + 2 * p, WIN + 2 * p + 1)
             near = (
                 with_halo(done[0], from_left[c], low[:1]),
@@ -289,61 +344,81 @@
                 with_halo(done[2], from_right[c], high[:1]),
                 with_halo(done[3], from_right[c], high),
             )
-            resid = [
-                (mine[h, i, :, lane : lane + widths[c]].astype(F32) - t * PTS ** (-0.5)).astype(BF16)
-                for i, t in zip(done, near)
-            ]
-            inner = [mm(inv[i], r) for i, r in zip(done, resid)]
-            for i, z in zip(done, inner):
-                out[pl.ds(i * PTS, PTS), cols] = z
-            for i, z in zip(done, inner):
-                up[c][pl.ds(i * SK, SK), :] = mm(leaf_pick[i], z.astype(BF16)).astype(BF16)
-
-    def gather(c):
-        return [
-            pltpu.make_async_remote_copy(
-                src_ref=top[c],
-                dst_ref=gath[c].at[pl.ds(pl.multiple_of(tx * nodes * SK, SK), nodes * SK), :],
-                send_sem=top_send.at[c, k - 1],
-                recv_sem=top_recv.at[c, k - 1],
-                device_id=(lax.rem(tx + k, n_tx), ty),
-                device_id_type=MESH,
-            )
-            for k in range(1, n_tx)
-        ]
+            resid = finish(done, near)
+            if pieces[c] > 1:
+                inverse(done, resid)
+            else:
+                for i, r in zip(done, resid):
+                    held[i, :, : widths[c]] = r
+        if pieces[c] == 1:
+
+            def group(g, _):
+                done = [g * 4 + k for k in range(4)]
+                inverse(done, [held[i, :, : widths[c]] for i in done])
+                return 0
+
+            lax.fori_loop(0, leaves // 4, group, 0)
+
+    def top_copy(c, src, owner, sem, t):
+        return pltpu.make_async_remote_copy(
+            src_ref=src,
+            dst_ref=gath[c].at[rows_of(owner, nodes * SK)],
+            send_sem=top_send.at[c, sem],
+            recv_sem=top_recv.at[c, sem],
+            device_id=(t, ty),
+            device_id_type=MESH,
+        )
+
+    def far_copies(c):
+        return [top_copy(c, top[c], tx, k, lax.rem(tx + 2 * k, n_tx)) for k in range(1, turns)]
+
+    def near_copy(c):
+        return top_copy(c, top[c], tx, 0, mate)
+
+    def second_copies(c):
+        copies = []
+        for k in range(1, turns):
+            owner = lax.rem(tx + n_tx - 2 * k, n_tx)
+            block = gath[c].at[rows_of(owner, nodes * SK)]
+            copies.append(top_copy(c, block, owner, turns - 1 + k, mate))
+        return copies
 
     def send_top(c):
         for n in range(nodes):
             block = mm(node_pick[n], up[c][pl.ds(n * node_rows, node_rows), :]).astype(BF16)
             top[c][pl.ds(n * SK, SK), :] = block
             gath[c][pl.ds(pl.multiple_of(tx * nodes * SK + n * SK, SK), SK), :] = block
-        for copy in gather(c):
+        for copy in far_copies(c):
             copy.start()
-
-    def downward(c):
+        near_copy(c).start()
+
+    def pass_on(c):
+        for first, second in zip(far_copies(c), second_copies(c)):
+            first.wait_recv()
+            second.start()
+
+    def gathered(c):
+        for copy in far_copies(c):
+            copy.wait_send()
+        near_copy(c).wait()
+        for copy in second_copies(c):
+            copy.wait()
+
+    def correct(c):
         cols = pl.ds(starts[c], widths[c])
-        for copy in gather(c):
-            copy.wait()
-        back = mm(coup_rows[...], gath[c][...])
-        for n in range(nodes):
-            part = back[n * SK : (n + 1) * SK]
-            high = part.astype(BF16)
-            low = (part - high.astype(F32)).astype(BF16)
-            spread = mm(node_spread[n], high) + mm(node_spread[n], low)
-            here = up[c][pl.ds(n * node_rows, node_rows), :].astype(F32)
-            down = (here - spread).astype(BF16)
-            coup = mm(lone[n], down).astype(BF16)
-            for j in range(GROUP):
-                i = n * GROUP + j
-                rows = pl.ds(i * PTS, PTS)
-                out[rows, cols] = out[rows, cols] - mm(
-                    inv_cols[i], coup[j * SK : (j + 1) * SK]
-                )
+
+        def store(i, x):
+            rows = pl.ds(i * PTS, PTS)
+            out[rows, cols] = out[rows, cols] - x
+
+        gathered(c)
+        downward(nodes, coup_rows, gath[c], up[c], node_spread, lone, inv_cols, store)
 
     for h in range(halves):
         own(h).wait()
     for h in range(halves):
         own_near(h)
+    last = chunks - 1
     for c in range(chunks):
         upward(c)
         send_top(c)
@@ -351,8 +426,33 @@
             loads[1].wait()
             loads[2].wait()
         else:
-            downward(c - 1)
-    downward(chunks - 1)
+            correct(c - 1)
+    pass_on(last)
+    gathered(last)
+
+
+def last_kernel(nodes, start, held, gath, up, coup_rows, lone, node_spread, inv_cols, out, sol, sem):
+    ready = pltpu.make_async_copy(
+        held.at[:, pl.ds(0, start)], out.at[:, pl.ds(0, start)], sem.at[nodes]
+    )
+    ready.start()
+    width = held.shape[1] - start
+    part = held.shape[0] // nodes
+
+    def done(n):
+        rows = pl.ds(n * part, part)
+        return pltpu.make_async_copy(sol.at[rows], out.at[rows, pl.ds(start, width)], sem.at[n])
+
+    def store(i, x):
+        rows = pl.ds(i * PTS, PTS)
+        sol[rows, :] = held[rows, pl.ds(start, width)] - x
+        if (i + 1) % GROUP == 0:
+            done(i // GROUP).start()
+
+    downward(nodes, coup_rows, gath, up, node_spread, lone, inv_cols, store)
+    ready.wait()
+    for n in range(nodes):
+        done(n).wait()
 
 
 def on_device(rhs, pts, leaf_inv, level_one, coupling, neigh, counts, leaf_skel, node_skel):
@@ -365,22 +465,20 @@
     side = WIN * PTS
     halves = cols // WIDE
     dma = pltpu.SemaphoreType.DMA
+    tops = n_tx * nodes * SK
     scratch = (
         [pltpu.VMEM((WIN, PTS, w), BF16) for w in widths * 2]
-        + [pltpu.VMEM((leaves * SK, w), BF16) for w in widths]
-        + [pltpu.VMEM((n_tx * nodes * SK, w), BF16) for w in widths]
         + [pltpu.VMEM((nodes * SK, w), BF16) for w in widths]
+        + [pltpu.VMEM((leaves * SK, w), BF16) for w in widths[:-1]]
+        + [pltpu.VMEM((tops, w), BF16) for w in widths[:-1]]
         + [
             pltpu.VMEM((halves, leaves + 1, PTS, WIDE), BF16),
+            pltpu.VMEM((leaves, PTS, WIDE), BF16),
             pltpu.SMEM((leaves * WIN,), jnp.int32),
             pltpu.VMEM((leaves * NBR + 1, PTS, PTS), BF16),
             pltpu.VMEM(leaf_inv.shape, BF16),
-            pltpu.VMEM(level_one.shape, BF16),
-            pltpu.VMEM(coupling.shape[1:], BF16),
-            pltpu.VMEM((leaves, PTS, SK), BF16),
             pltpu.VMEM((leaves, SK, PTS), BF16),
             pltpu.VMEM((nodes, SK, GROUP * SK), BF16),
-            pltpu.VMEM((nodes, GROUP * SK, SK), BF16),
             pltpu.VMEM((2 * DIM, side // 2), BF16),
             pltpu.VMEM((2 * DIM, side // 2), BF16),
             pltpu.VMEM((2 * DIM, side // 2), BF16),
@@ -401,19 +499,49 @@
     vmem = pl.BlockSpec(memory_space=pltpu.VMEM)
     smem = pl.BlockSpec(memory_space=pltpu.SMEM)
     hbm = pl.BlockSpec(memory_space=pltpu.HBM)
-    return pl.pallas_call(
+    kept = (
+        pltpu.VMEM((rows, cols), F32),
+        pltpu.VMEM((tops, widths[-1]), BF16),
+        pltpu.VMEM((leaves * SK, widths[-1]), BF16),
+        pltpu.VMEM(coupling.shape[1:], BF16),
+        pltpu.VMEM(level_one.shape, BF16),
+        pltpu.VMEM((nodes, GROUP * SK, 2 * SK), BF16),
+        pltpu.VMEM((leaves // 2, PTS, 2 * SK), BF16),
+    )
+    parts = pl.pallas_call(
         functools.partial(device_kernel, (leaves, nodes, widths, pieces, n_tx, n_ty)),
-        out_shape=pltpu.VMEM((rows, cols), F32),
+        out_shape=kept,
         in_specs=[hbm, vmem, hbm, hbm, hbm, smem, smem, vmem, vmem],
-        out_specs=vmem,
+        out_specs=(vmem,) * len(kept),
         scratch_shapes=scratch,
         compiler_params=pltpu.CompilerParams(
-            collective_id=0, has_side_effects=True, vmem_limit_bytes=50 * 2**20
+            collective_id=0, has_side_effects=True, vmem_limit_bytes=42 * 2**20
         ),
         cost_estimate=pl.CostEstimate(
             flops=2 * 6_500_000_000, bytes_accessed=20_000_000, transcendentals=8_400_000
         ),
-    )(rhs.reshape(leaves, PTS, cols), pts, leaf_inv, level_one, coupling, neigh.T, counts, leaf_skel, node_skel)
+    )(
+        rhs.reshape(leaves, PTS, cols),
+        pts,
+        leaf_inv,
+        level_one,
+        coupling,
+        neigh.T,
+        counts,
+        leaf_skel,
+        node_skel,
+    )
+    return pl.pallas_call(
+        functools.partial(last_kernel, nodes, cols - widths[-1]),
+        out_shape=jax.ShapeDtypeStruct((rows, cols), F32),
+        in_specs=[vmem] * len(kept),
+        out_specs=hbm,
+        scratch_shapes=[pltpu.VMEM((rows, widths[-1]), F32), dma((nodes + 1,))],
+        compiler_params=pltpu.CompilerParams(vmem_limit_bytes=16 * 2**20),
+        cost_estimate=pl.CostEstimate(
+            flops=2 * 250_000_000, bytes_accessed=8_400_000, transcendentals=0
+        ),
+    )(*parts)
 
 
 def solution(mesh):

time: 82.8 us -> 75.7 us (0.914)
  Pallas kernels: 79.3 us -> 75.4 us
  local copies, waits for them, and re-layouts: 3.4 us -> 0 us
    pallas_call x1, Pallas kernels: 79.3 us -> 70.8 us  [on_device(): pl.pallas_call(functools.partial(device_kernel, (leaves, nodes, widths, p...]
    pallas_call x0 -> x1, Pallas kernels: none -> 4.6 us  [on_device(): pl.pallas_call(functools.partial(last_kernel, nodes, cols - widths[-1]),...]
    unnamed x1 -> x0, local copies, waits for them, and re-layouts: 3.4 us -> none
where the time goes in v2:
time: 75.7 us; the launch traced here: 75.6 us
  Pallas kernels  75.4 us (100%)
    pallas_call x1, Pallas kernels, on_device(): pl.pallas_call(functools.partial(device_kernel, (leaves, nodes, widths, p...  70.8 us
    pallas_call x1, Pallas kernels, on_device(): pl.pallas_call(functools.partial(last_kernel, nodes, cols - widths[-1]),...  4.6 us

profile of v2, /device:TPU:1, one launch (start us, length us, event | category | flops | bytes accessed | tf_op | source)
XLA Modules:
  0.0 75.6 jit_solution(4579250501819687282)
XLA Ops:
  0.0 70.8 %shard_map.91 = (f32[4096,512]{1,0:T(8,128)S(1)}, bf16[2048,128]{1,0:T(8,128)(2,1)S(1)}, bf16[2048,128]{1,0:T(8,128)(2,1)S(1)}, bf16[256,2048]{1,0:T(8,128)(2,1)...) custom-call(bf16[16,256,512]{2,1,0:T(8,128)(2,1)} %bitcast.2, ...), custom_call_target="tpu_custom_call" | custom-call | flops 12999999488 | bytes 20000000 | tf_op jit(solution)/shard_map/pallas_call | solution.py:511
  70.8 4.6 %shard_map.92 = f32[4096,512]{1,0:T(8,128)} custom-call(f32[4096,512]{1,0:T(8,128)S(1)} %get-tuple-element.12.held, bf16[2048,128]{1,0:T(8,128)(2,1)S(1)} %get-tuple-element.13.gath, bf16[2048,128]{1,0:T(8,128)(2,1)S(1)} %get-tuple-element.14.up, bf16[256,2048]{1,0:T(8,128)(2,1)S(1)} %get-tuple-element.15.coup_rows, ...), custom_call_target="tpu_custom_call" | custom-call | flops 500000000 | bytes 8400000 | tf_op jit(solution)/shard_map/pallas_call | solution.py:534

commit v3 on v2

--- a/solution.py
+++ b/solution.py
@@ -29,11 +29,12 @@
     return pl.ds(pl.multiple_of(i * size, size), size)
 
 
-def downward(nodes, coup_rows, gath, up, node_spread, lone, inv_cols, store):
+def downward(which, coup_rows, gath, up, node_spread, lone, inv_cols, store):
     width = up.shape[1]
-    back = mm(coup_rows[...], gath[...])
-    for n in range(nodes):
-        part = back[n * SK : (n + 1) * SK]
+    first = which[0]
+    back = mm(coup_rows[first * SK : (which[-1] + 1) * SK, :], gath[...])
+    for n in which:
+        part = back[(n - first) * SK : (n - first + 1) * SK]
         high = part.astype(BF16)
         low = (part - high.astype(F32)).astype(BF16)
         spread = mm(node_spread[n], jnp.concatenate([high, low], axis=0))
@@ -128,6 +129,7 @@
         pl.semaphore_signal(barrier, inc=1, device_id=(tx, t), device_id_type=MESH)
     mate = tx + 1 - 2 * lax.rem(tx, 2)
     turns = n_tx // 2
+    hops = (*(k for k in range(1, turns) if 2 * k != turns), turns // 2)
     for t in [mate] + [lax.rem(tx + 2 * k, n_tx) for k in range(1, turns)]:
         pl.semaphore_signal(barrier, inc=1, device_id=(t, ty), device_id_type=MESH)
     pl.semaphore_wait(barrier, 2 + turns)
@@ -189,6 +191,8 @@
         pltpu.make_async_copy(level_one, lone, load_sem.at[2]),
     )
 
+    for copy in halo(0, 0):
+        copy.start()
     coords = pts[...].astype(F32)
 
     def two_rows(x):
@@ -199,7 +203,7 @@
     for copy in points_halo():
         copy.start()
     for c in range(chunks):
-        for p in range(pieces[c]):
+        for p in range(0 if c else 1, pieces[c]):
             for copy in halo(c, p):
                 copy.start()
     for copy in loads:
@@ -295,7 +299,7 @@
             out[rows_of(i, PTS), cols] = total
             return 0
 
-        lax.fori_loop(0, leaves, leaf, 0, unroll=4)
+        lax.fori_loop(0, leaves, leaf, 0, unroll=8)
 
     def upward(c):
         cols = pl.ds(starts[c], widths[c])
@@ -319,12 +323,12 @@
                 up[c][rows_of(i, SK), :] = mm(leaf_pick[i], z.astype(BF16)).astype(BF16)
 
         for p in range(WIN // 2):
+            if c > 0 and p == (0 if c < chunks - 1 else WIN // 2 - 2):
+                pass_on(c - 1, hops)
             step = WIN // 2 // pieces[c]
             if p % step == 0:
                 for copy in halo(c, p // step):
                     copy.wait()
-            if c > 0 and p == (0 if pieces[c] == 1 else WIN // 2 - 2):
-                pass_on(c - 1)
             low, high = (WIN - 1 - 2 * p, WIN - 2 - 2 * p), (2 * p, 2 * p + 1)
 
             def leaf(i, _):
@@ -345,19 +349,19 @@
                 with_halo(done[3], from_right[c], high),
             )
             resid = finish(done, near)
-            if pieces[c] > 1:
+            if c == chunks - 1:
                 inverse(done, resid)
             else:
                 for i, r in zip(done, resid):
                     held[i, :, : widths[c]] = r
-        if pieces[c] == 1:
+        if c < chunks - 1:
 
             def group(g, _):
                 done = [g * 4 + k for k in range(4)]
                 inverse(done, [held[i, :, : widths[c]] for i in done])
                 return 0
 
-            lax.fori_loop(0, leaves // 4, group, 0)
+            lax.fori_loop(0, leaves // 4, group, 0, unroll=2)
 
     def top_copy(c, src, owner, sem, t):
         return pltpu.make_async_remote_copy(
@@ -369,50 +373,46 @@
             device_id_type=MESH,
         )
 
-    def far_copies(c):
-        return [top_copy(c, top[c], tx, k, lax.rem(tx + 2 * k, n_tx)) for k in range(1, turns)]
+    def far_copy(c, k):
+        return top_copy(c, top[c], tx, k, lax.rem(tx + 2 * k, n_tx))
 
     def near_copy(c):
         return top_copy(c, top[c], tx, 0, mate)
 
-    def second_copies(c):
-        copies = []
-        for k in range(1, turns):
-            owner = lax.rem(tx + n_tx - 2 * k, n_tx)
-            block = gath[c].at[rows_of(owner, nodes * SK)]
-            copies.append(top_copy(c, block, owner, turns - 1 + k, mate))
-        return copies
+    def second_copy(c, k):
+        owner = lax.rem(tx + n_tx - 2 * k, n_tx)
+        block = gath[c].at[rows_of(owner, nodes * SK)]
+        return top_copy(c, block, owner, turns - 1 + k, mate)
 
     def send_top(c):
         for n in range(nodes):
             block = mm(node_pick[n], up[c][pl.ds(n * node_rows, node_rows), :]).astype(BF16)
             top[c][pl.ds(n * SK, SK), :] = block
             gath[c][pl.ds(pl.multiple_of(tx * nodes * SK + n * SK, SK), SK), :] = block
-        for copy in far_copies(c):
-            copy.start()
+        for k in hops:
+            far_copy(c, k).start()
         near_copy(c).start()
 
-    def pass_on(c):
-        for first, second in zip(far_copies(c), second_copies(c)):
-            first.wait_recv()
-            second.start()
+    def pass_on(c, which):
+        for k in which:
+            far_copy(c, k).wait_recv()
+            second_copy(c, k).start()
 
     def gathered(c):
-        for copy in far_copies(c):
-            copy.wait_send()
+        for k in hops:
+            far_copy(c, k).wait_send()
         near_copy(c).wait()
-        for copy in second_copies(c):
-            copy.wait()
-
-    def correct(c):
+        for k in hops:
+            second_copy(c, k).wait()
+
+    def correct(c, which):
         cols = pl.ds(starts[c], widths[c])
 
         def store(i, x):
             rows = pl.ds(i * PTS, PTS)
             out[rows, cols] = out[rows, cols] - x
 
-        gathered(c)
-        downward(nodes, coup_rows, gath[c], up[c], node_spread, lone, inv_cols, store)
+        downward(which, coup_rows, gath[c], up[c], node_spread, lone, inv_cols, store)
 
     for h in range(halves):
         own(h).wait()
@@ -422,37 +422,44 @@
     for c in range(chunks):
         upward(c)
         send_top(c)
-        if c == 0:
-            loads[1].wait()
-            loads[2].wait()
-        else:
-            correct(c - 1)
-    pass_on(last)
+    loads[1].wait()
+    loads[2].wait()
+    for c in range(last):
+        gathered(c)
+    for c in range(last - 1):
+        correct(c, range(nodes))
+    pass_on(last, hops[:-1])
+    for n in range(nodes):
+        if n == nodes - 1:
+            pass_on(last, hops[-1:])
+        correct(last - 1, range(n, n + 1))
     gathered(last)
 
 
 def last_kernel(nodes, start, held, gath, up, coup_rows, lone, node_spread, inv_cols, out, sol, sem):
-    ready = pltpu.make_async_copy(
-        held.at[:, pl.ds(0, start)], out.at[:, pl.ds(0, start)], sem.at[nodes]
-    )
-    ready.start()
     width = held.shape[1] - start
-    part = held.shape[0] // nodes
-
-    def done(n):
-        rows = pl.ds(n * part, part)
-        return pltpu.make_async_copy(sol.at[rows], out.at[rows, pl.ds(start, width)], sem.at[n])
+    part = held.shape[0] // (2 * nodes)
+
+    def ready(b):
+        here = (pl.ds(b * part, part), pl.ds(0, start))
+        return pltpu.make_async_copy(held.at[here], out.at[here], sem.at[0, b])
+
+    def done(b):
+        rows = pl.ds(b * part, part)
+        return pltpu.make_async_copy(sol.at[rows], out.at[rows, pl.ds(start, width)], sem.at[1, b])
 
     def store(i, x):
         rows = pl.ds(i * PTS, PTS)
         sol[rows, :] = held[rows, pl.ds(start, width)] - x
-        if (i + 1) % GROUP == 0:
-            done(i // GROUP).start()
-
-    downward(nodes, coup_rows, gath, up, node_spread, lone, inv_cols, store)
-    ready.wait()
-    for n in range(nodes):
-        done(n).wait()
+        if (i + 1) % (GROUP // 2) == 0:
+            done(i // (GROUP // 2)).start()
+
+    for b in range(2 * nodes):
+        ready(b).start()
+    downward(range(nodes), coup_rows, gath, up, node_spread, lone, inv_cols, store)
+    for b in range(2 * nodes):
+        ready(b).wait()
+        done(b).wait()
 
 
 def on_device(rhs, pts, leaf_inv, level_one, coupling, neigh, counts, leaf_skel, node_skel):
@@ -460,7 +467,7 @@
     leaves, nodes = leaf_inv.shape[0], level_one.shape[0]
     n_tx, n_ty = lax.axis_size("tx"), lax.axis_size("ty")
     widths = (WIDE,) * (cols // WIDE - 1) + (WIDE // 2,) * 2
-    pieces = (1,) * (len(widths) - 1) + (4,)
+    pieces = (4,) + (1,) * (len(widths) - 2) + (4,)
     chunks = len(widths)
     side = WIN * PTS
     halves = cols // WIDE
@@ -536,7 +543,10 @@
         out_shape=jax.ShapeDtypeStruct((rows, cols), F32),
         in_specs=[vmem] * len(kept),
         out_specs=hbm,
-        scratch_shapes=[pltpu.VMEM((rows, widths[-1]), F32), dma((nodes + 1,))],
+        scratch_shapes=[
+            pltpu.VMEM((rows, widths[-1]), F32),
+            dma((2, 2 * nodes)),
+        ],
         compiler_params=pltpu.CompilerParams(vmem_limit_bytes=16 * 2**20),
         cost_estimate=pl.CostEstimate(
             flops=2 * 250_000_000, bytes_accessed=8_400_000, transcendentals=0

time: 75.7 us -> 72.5 us (0.958)
  Pallas kernels: 75.4 us -> 72.2 us
    pallas_call x1, Pallas kernels: 70.8 us -> 67.7 us  [on_device(): pl.pallas_call(functools.partial(device_kernel, (leaves, nodes, widths, p...]
where the time goes in v3:
time: 72.5 us; the launch traced here: 72.4 us
  Pallas kernels  72.2 us (100%)
    pallas_call x1, Pallas kernels, on_device(): pl.pallas_call(functools.partial(device_kernel, (leaves, nodes, widths, p...  67.7 us
    pallas_call x1, Pallas kernels, on_device(): pl.pallas_call(functools.partial(last_kernel, nodes, cols - widths[-1]),...  4.5 us

profile of v3, /device:TPU:1, one launch (start us, length us, event | category | flops | bytes accessed | tf_op | source)
XLA Modules:
  0.0 72.4 jit_solution(381833744439868898)
XLA Ops:
  0.0 67.7 %shard_map.91 = (f32[4096,512]{1,0:T(8,128)S(1)}, bf16[2048,128]{1,0:T(8,128)(2,1)S(1)}, bf16[2048,128]{1,0:T(8,128)(2,1)S(1)}, bf16[256,2048]{1,0:T(8,128)(2,1)...) custom-call(bf16[16,256,512]{2,1,0:T(8,128)(2,1)} %bitcast.2, ...), custom_call_target="tpu_custom_call" | custom-call | flops 12999999488 | bytes 20000000 | tf_op jit(solution)/shard_map/pallas_call | solution.py:518
  67.7 4.5 %shard_map.92 = f32[4096,512]{1,0:T(8,128)} custom-call(f32[4096,512]{1,0:T(8,128)S(1)} %get-tuple-element.12.held, bf16[2048,128]{1,0:T(8,128)(2,1)S(1)} %get-tuple-element.13.gath, bf16[2048,128]{1,0:T(8,128)(2,1)S(1)} %get-tuple-element.14.up, bf16[256,2048]{1,0:T(8,128)(2,1)S(1)} %get-tuple-element.15.coup_rows, ...), custom_call_target="tpu_custom_call" | custom-call | flops 500000000 | bytes 8400000 | tf_op jit(solution)/shard_map/pallas_call | solution.py:541

commit v4 on v3

--- a/solution.py
+++ b/solution.py
@@ -65,14 +65,14 @@
 def device_kernel(
     dims,
     rhs,
-    pts,
+    pts_in,
     leaf_inv,
     level_one,
     coupling,
-    neigh,
-    counts,
-    leaf_skel,
-    node_skel,
+    neigh_in,
+    counts_in,
+    leaf_skel_in,
+    node_skel_in,
     out,
     gath_last,
     up_last,
@@ -114,6 +114,12 @@
         top_recv,
         own_sem,
         load_sem,
+        pts,
+        leaf_skel,
+        node_skel,
+        neigh,
+        counts,
+        small_sem,
     ) = scratch
     tx = lax.axis_index("tx")
     ty = lax.axis_index("ty")
@@ -133,6 +139,15 @@
     for t in [mate] + [lax.rem(tx + 2 * k, n_tx) for k in range(1, turns)]:
         pl.semaphore_signal(barrier, inc=1, device_id=(t, ty), device_id_type=MESH)
     pl.semaphore_wait(barrier, 2 + turns)
+
+    small = [
+        pltpu.make_async_copy(a, b, small_sem.at[k])
+        for k, (a, b) in enumerate(
+            ((pts_in, pts), (leaf_skel_in, leaf_skel), (node_skel_in, node_skel), (neigh_in, neigh), (counts_in, counts),)
+        )
+    ]
+    for copy in small:
+        copy.start()
 
     def halo(c, p):
         cols = pl.ds(starts[c], widths[c])
@@ -193,6 +208,8 @@
 
     for copy in halo(0, 0):
         copy.start()
+    for copy in small:
+        copy.wait()
     coords = pts[...].astype(F32)
 
     def two_rows(x):
@@ -501,6 +518,12 @@
             dma((chunks, n_tx - 1)),
             dma((halves,)),
             dma((3,)),
+            pltpu.VMEM(pts.shape, BF16),
+            pltpu.VMEM(leaf_skel.shape, jnp.int32),
+            pltpu.VMEM(node_skel.shape, jnp.int32),
+            pltpu.SMEM(neigh.shape[::-1], jnp.int32),
+            pltpu.SMEM(counts.shape, jnp.int32),
+            dma((5,)),
         ]
     )
     vmem = pl.BlockSpec(memory_space=pltpu.VMEM)
@@ -518,7 +541,7 @@
     parts = pl.pallas_call(
         functools.partial(device_kernel, (leaves, nodes, widths, pieces, n_tx, n_ty)),
         out_shape=kept,
-        in_specs=[hbm, vmem, hbm, hbm, hbm, smem, smem, vmem, vmem],
+        in_specs=[hbm, hbm, hbm, hbm, hbm, hbm, hbm, hbm, hbm],
         out_specs=(vmem,) * len(kept),
         scratch_shapes=scratch,
         compiler_params=pltpu.CompilerParams(

time: 72.5 us -> 71.6 us (0.988)
  Pallas kernels: 72.2 us -> 71.3 us
    pallas_call x1, Pallas kernels: 67.7 us -> 66.8 us  [on_device(): pl.pallas_call(functools.partial(device_kernel, (leaves, nodes, widths, p...]
where the time goes in v4:
time: 71.6 us; the launch traced here: 71.5 us
  Pallas kernels  71.3 us (100%)
    pallas_call x1, Pallas kernels, on_device(): pl.pallas_call(functools.partial(device_kernel, (leaves, nodes, widths, p...  66.8 us
    pallas_call x1, Pallas kernels, on_device(): pl.pallas_call(functools.partial(last_kernel, nodes, cols - widths[-1]),...  4.5 us

profile of v4, /device:TPU:1, one launch (start us, length us, event | category | flops | bytes accessed | tf_op | source)
XLA Modules:
  0.0 71.5 jit_solution(2500324836501159163)
XLA Ops:
  0.0 66.8 %shard_map.91 = (f32[4096,512]{1,0:T(8,128)S(1)}, bf16[2048,128]{1,0:T(8,128)(2,1)S(1)}, bf16[2048,128]{1,0:T(8,128)(2,1)S(1)}, bf16[256,2048]{1,0:T(8,128)(2,1)...) custom-call(bf16[16,256,512]{2,1,0:T(8,128)(2,1)} %bitcast.2, ...), custom_call_target="tpu_custom_call" | custom-call | flops 12999999488 | bytes 20000000 | tf_op jit(solution)/shard_map/pallas_call | solution.py:541
  66.8 4.5 %shard_map.92 = f32[4096,512]{1,0:T(8,128)} custom-call(f32[4096,512]{1,0:T(8,128)S(1)} %get-tuple-element.12.held, bf16[2048,128]{1,0:T(8,128)(2,1)S(1)} %get-tuple-element.13.gath, bf16[2048,128]{1,0:T(8,128)(2,1)S(1)} %get-tuple-element.14.up, bf16[256,2048]{1,0:T(8,128)(2,1)S(1)} %get-tuple-element.15.coup_rows, ...), custom_call_target="tpu_custom_call" | custom-call | flops 500000000 | bytes 8400000 | tf_op jit(solution)/shard_map/pallas_call | solution.py:564
